TPU v7x, 32 devices: a whole 2x2x4 slice. The times are simulated.
32 devices in a mesh: fsdp: 2 (over x), heads: 4 (over z), tensor: 4 (over y, core).
Axes of the slice: x: 2, y: 2, z: 4, core: 2. Of those that a mesh axis runs over, the one named last changes fastest.
Arguments:
- tokens: bfloat16 [8, 256, 768], P(('fsdp', 'tensor')), may hold values from -6 to 6
- valid_mask: int32 [8, 256], P(('fsdp', 'tensor')), may hold values from 0 to 1, as said below
- routes: int32 [8, 256, 2], P('fsdp'), may hold values from 0 to 31, all different within a row; in each aligned block of 1024 rows (0 to 1023, 1024 to 2047, ..., all dimensions but the last counted through in order) at most 128 rows name the same one
- teacher: bfloat16 [8, 256, 768], P(('fsdp', 'tensor')), may hold values from -6 to 6
- gain_one: bfloat16 [768], P(('fsdp', 'tensor')), may hold values from 0.099609375 to 1.8984375
- qkv_weight: bfloat16 [768, 12, 192], P(('fsdp', 'tensor'), 'heads'), may hold values from -0.3125 to 0.3125
- out_weight: bfloat16 [12, 64, 768], P('heads', None, ('fsdp', 'tensor')), may hold values from -1 to 1
- gain_two: bfloat16 [768], P(('fsdp', 'tensor')), may hold values from 0.099609375 to 1.8984375
- router_weight: bfloat16 [768, 32], P(('fsdp', 'tensor')), may hold values from -0.109375 to 0.109375
- expert_up: bfloat16 [32, 768, 3072], P('heads', 'fsdp', 'tensor'), may hold values from -0.21875 to 0.21875
- expert_down: bfloat16 [32, 3072, 768], P('heads', 'tensor', 'fsdp'), may hold values from -3.5 to 3.5
Outputs:
- result: bfloat16 [8, 256, 768], P(('fsdp', 'tensor'))
- loss_terms: float32 [8], P(('fsdp', 'tensor'))
- tokens_grad: float32 [8, 256, 768], P(('fsdp', 'tensor'))
- gain_one_grad: float32 [768], P(('fsdp', 'tensor'))
- qkv_grad: float32 [768, 12, 192], P(('fsdp', 'tensor'), 'heads')
- out_weight_grad: float32 [12, 64, 768], P('heads', None, ('fsdp', 'tensor'))
- gain_two_grad: float32 [768], P(('fsdp', 'tensor'))
- router_grad: float32 [768, 32], P(('fsdp', 'tensor'))
- expert_up_grad: float32 [32, 768, 3072], P('heads', 'fsdp', 'tensor')
- expert_down_grad: float32 [32, 3072, 768], P('heads', 'tensor', 'fsdp')
Inputs may be any that keep to these rules, and one draw needn't show every extreme that they name: `valid_mask`: an image's valid tokens are its first ones, 1 to 197 of them; some image has exactly 197. `routes`: each row names 2 different experts. In the 1024 rows of each index of fsdp no expert is named more than 128 times, a bound that some block reaches.
All inputs are finite; a program needn't handle non-finite values.
Results may differ from a plain program's by a relative error of at most 0.012.
The roundings to bfloat16 on the way count: a program that leaves them out, or rounds other values in their place, can miss the bound.
Values may be sent and summed in bfloat16 or wider, within the bound.
A program may use at most 192 MiB of HBM per device.

v0:
```python
import jax
import jax.numpy as jnp
from jax import lax
from jax.sharding import PartitionSpec as P

EPSILON = 1e-06
MASKED = -1e30
ROOT_HALF = 0.7071067811865476
DENSITY = 0.3989422804014327


def normalize(values):
    center = values - jnp.mean(values, -1, keepdims=True)
    inv_std = lax.rsqrt(jnp.mean(center * center, -1, keepdims=True) + EPSILON)
    return (center * inv_std, inv_std)


def norm_back(gradient, normed, inv_std, gain_vector):
    weighted = gradient * gain_vector
    gain_grad = jnp.sum(gradient * normed, axis=(0, 1))
    inner = (
        weighted
        - jnp.mean(weighted, -1, keepdims=True)
        - normed * jnp.mean(weighted * normed, -1, keepdims=True)
    )
    return (inner * inv_std, gain_grad)


def scores_of(queries, key_rows, keys_ok, score_scale):
    raw_scores = (
        jnp.einsum("iqhe,ikhe->ihqk", queries, key_rows, preferred_element_type=jnp.float32)
        * score_scale
    )
    return jnp.where(keys_ok, raw_scores, MASKED)


def gather_weights(
    gain_one, qkv_weight, out_weight, gain_two, router_weight, expert_up, expert_down
):
    dense_set = (
        lax.all_gather(qkv_weight, ("fsdp", "tensor"), axis=0, tiled=True),
        lax.all_gather(out_weight, ("fsdp", "tensor"), axis=2, tiled=True),
        lax.all_gather(router_weight, ("fsdp", "tensor"), axis=0, tiled=True),
        lax.all_gather(gain_one, ("fsdp", "tensor"), axis=0, tiled=True),
        lax.all_gather(gain_two, ("fsdp", "tensor"), axis=0, tiled=True),
    )
    expert_set = (
        lax.all_gather(expert_up, "fsdp", axis=1, tiled=True),
        lax.all_gather(expert_down, "fsdp", axis=2, tiled=True),
    )
    return (dense_set, expert_set)


def reduce_expert_grads(up_grad, down_grad):
    return (
        lax.psum_scatter(up_grad, "fsdp", scatter_dimension=1, tiled=True),
        lax.psum_scatter(down_grad, "fsdp", scatter_dimension=2, tiled=True),
    )


def local(
    tokens,
    valid_mask,
    routes,
    teacher,
    gain_one,
    qkv_weight,
    out_weight,
    gain_two,
    router_weight,
    expert_up,
    expert_down,
):
    valid_total = lax.psum(jnp.sum(valid_mask.astype(jnp.float32)), ("fsdp", "tensor"))
    dense_set, expert_set = gather_weights(
        gain_one, qkv_weight, out_weight, gain_two, router_weight, expert_up, expert_down
    )
    qkv_full, output_complete, router_full, gain_a, gain_b = dense_set
    up_full, down_full = expert_set
    image_count, token_slots, model_width = tokens.shape
    head_dim = qkv_full.shape[2] // 3
    local_experts = expert_up.shape[0]
    tensor_size = lax.axis_size("tensor")
    group_images = image_count * tensor_size
    group_rows = group_images * token_slots
    top_choices = routes.shape[2]
    expert_count = local_experts * lax.axis_size("heads")
    capacity = 2 * top_choices * group_rows // expert_count
    slot_count = local_experts * capacity
    total_tokens = image_count * token_slots * lax.axis_size("fsdp") * tensor_size
    total_images = image_count * lax.axis_size("fsdp") * tensor_size
    score_scale = head_dim ** (-0.5)
    inputs = tokens.astype(jnp.float32)
    normed_one, spread_one = normalize(inputs)
    first_in = (normed_one * gain_a.astype(jnp.float32)).astype(jnp.bfloat16)
    projected = jnp.einsum(
        "isd,dhe->ishe", first_in, qkv_full, preferred_element_type=jnp.float32
    ).astype(jnp.bfloat16)
    queries = projected[..., :head_dim]
    key_rows = projected[..., head_dim : 2 * head_dim]
    values = projected[..., 2 * head_dim :]
    keys_ok = (valid_mask > 0)[:, None, None, :]
    scores = scores_of(queries, key_rows, keys_ok, score_scale)
    peak_score = jnp.max(scores, -1, keepdims=True)
    exp_scores = jnp.exp(scores - peak_score)
    score_total = jnp.sum(exp_scores, -1, keepdims=True)
    logarithm_total = peak_score + jnp.log(score_total)
    attention = (exp_scores / score_total).astype(jnp.bfloat16)
    combined_heads = jnp.einsum(
        "ihqk,ikhe->iqhe", attention, values, preferred_element_type=jnp.float32
    ).astype(jnp.bfloat16)
    attn_part = jnp.einsum(
        "iqhe,hed->iqd", combined_heads, output_complete, preferred_element_type=jnp.float32
    )
    attended = lax.psum(attn_part, "heads")
    residual = inputs + attended
    normed_two, spread_two = normalize(residual)
    second_in = (normed_two * gain_b.astype(jnp.float32)).astype(jnp.bfloat16)
    group_in = lax.all_gather(second_in, "tensor", axis=0, tiled=True)
    rows_in = group_in.reshape(group_rows, model_width)
    logits = jnp.dot(rows_in, router_full, preferred_element_type=jnp.float32)
    peak_logit = jnp.max(logits, -1, keepdims=True)
    exponent_logits = jnp.exp(logits - peak_logit)
    router_probs = exponent_logits / jnp.sum(exponent_logits, -1, keepdims=True)
    expert_ids = jnp.arange(expert_count, dtype=jnp.int32)
    route_pairs = routes.reshape(group_rows, top_choices)
    picked_hot = (route_pairs[:, :, None] == expert_ids[None, None, :]).astype(jnp.float32)
    gate_weight_values = jnp.sum(router_probs[:, None, :] * picked_hot, -1)
    flat_routes = route_pairs.reshape(group_rows * top_choices)
    route_hot = (flat_routes[:, None] == expert_ids[None, :]).astype(jnp.int32)
    earlier = jnp.cumsum(route_hot, 0) - route_hot
    slot_index = jnp.sum(earlier * route_hot, 1)
    first_expert = lax.axis_index("heads") * local_experts
    is_local = (flat_routes >= first_expert) & (flat_routes < first_expert + local_experts)
    target = jnp.where(is_local, (flat_routes - first_expert) * capacity + slot_index, slot_count)
    owner_row = jnp.arange(group_rows * top_choices, dtype=jnp.int32) // top_choices
    source = jnp.zeros((slot_count,), jnp.int32).at[target].set(owner_row, mode="drop")
    slot_gate = (
        jnp.zeros((slot_count,), jnp.float32)
        .at[target]
        .set(gate_weight_values.reshape(-1), mode="drop")
    )
    slot_pick = jnp.minimum(target, slot_count - 1)
    retain_mask = is_local.astype(jnp.float32)
    dispatched = rows_in[source].reshape(local_experts, capacity, model_width)
    before_gelu = jnp.einsum(
        "ecd,edf->ecf", dispatched, up_full, preferred_element_type=jnp.float32
    )
    hidden = jax.nn.gelu(before_gelu, approximate=False).astype(jnp.bfloat16)
    expert_out = jnp.einsum(
        "ecf,efd->ecd", hidden, down_full, preferred_element_type=jnp.float32
    ).reshape(slot_count, model_width)
    weighted = expert_out * slot_gate[:, None]
    moe_part = jnp.sum(
        (weighted[slot_pick] * retain_mask[:, None]).reshape(group_rows, top_choices, model_width),
        1,
    )
    moe_part = moe_part.reshape(group_images, token_slots, model_width)
    expert_sum = lax.psum(
        lax.psum_scatter(moe_part, "tensor", scatter_dimension=0, tiled=True), "heads"
    )
    final = residual + expert_sum
    valid_rows = valid_mask.astype(jnp.float32)[..., None]
    difference = (final - teacher.astype(jnp.float32)) * valid_rows
    loss_terms = jnp.sum(difference * difference, axis=(1, 2)) * (
        total_images / (valid_total * model_width)
    )
    final_grad = difference * (total_tokens / valid_total)
    dense_set, expert_set = gather_weights(
        gain_one, qkv_weight, out_weight, gain_two, router_weight, expert_up, expert_down
    )
    qkv_full, output_complete, router_full, gain_a, gain_b = dense_set
    up_full, down_full = expert_set
    moe_grad = final_grad.astype(jnp.bfloat16)
    group_grad = lax.all_gather(moe_grad, "tensor", axis=0, tiled=True).reshape(
        group_rows, model_width
    )
    slot_grad = group_grad[source].astype(jnp.float32)
    gate_slot_grad = jnp.sum(slot_grad * expert_out, -1)
    out_grad = (
        (slot_grad * slot_gate[:, None])
        .astype(jnp.bfloat16)
        .reshape(local_experts, capacity, model_width)
    )
    expert_down_grad = jnp.einsum(
        "ecf,ecd->efd", hidden, out_grad, preferred_element_type=jnp.float32
    )
    hidden_grad = jnp.einsum(
        "ecd,efd->ecf", out_grad, down_full, preferred_element_type=jnp.float32
    )
    normal_cdf = 0.5 * (1.0 + lax.erf(before_gelu * ROOT_HALF))
    slope = normal_cdf + before_gelu * DENSITY * jnp.exp(-0.5 * before_gelu * before_gelu)
    pre_grad = (hidden_grad * slope).astype(jnp.bfloat16)
    expert_up_grad = jnp.einsum(
        "ecd,ecf->edf", dispatched, pre_grad, preferred_element_type=jnp.float32
    )
    row_grad = jnp.einsum(
        "ecf,edf->ecd", pre_grad, up_full, preferred_element_type=jnp.float32
    ).reshape(slot_count, model_width)
    rows_part = jnp.sum(
        (row_grad[slot_pick] * retain_mask[:, None]).reshape(group_rows, top_choices, model_width),
        1,
    )
    rows_part = rows_part.reshape(group_images, token_slots, model_width)
    gate_part = (gate_slot_grad[slot_pick] * retain_mask).reshape(
        group_images, token_slots, top_choices
    )
    rows_share, gate_share = (
        lax.psum_scatter(rows_part, "tensor", scatter_dimension=0, tiled=True),
        lax.psum_scatter(gate_part, "tensor", scatter_dimension=0, tiled=True),
    )
    second_grad, gate_grad = lax.psum((rows_share, gate_share), "heads")
    own_start = lax.axis_index("tensor") * image_count * token_slots
    own_rows = image_count * token_slots
    own_probs = lax.dynamic_slice_in_dim(router_probs, own_start, own_rows, 0).reshape(
        image_count, token_slots, expert_count
    )
    own_hot = lax.dynamic_slice_in_dim(picked_hot, own_start, own_rows, 0).reshape(
        image_count, token_slots, top_choices, expert_count
    )
    prob_grad = jnp.sum(gate_grad[..., None] * own_hot, 2)
    logit_grad = (
        own_probs * (prob_grad - jnp.sum(own_probs * prob_grad, -1, keepdims=True))
    ).astype(jnp.bfloat16)
    router_grad = jnp.einsum(
        "isd,ise->de", second_in, logit_grad, preferred_element_type=jnp.float32
    )
    second_grad = second_grad + jnp.einsum(
        "ise,de->isd", logit_grad, router_full, preferred_element_type=jnp.float32
    )
    residual_norm, gain_two_grad = norm_back(
        second_grad, normed_two, spread_two, gain_b.astype(jnp.float32)
    )
    residual_grad = final_grad + residual_norm
    attended_output_gradient = residual_grad.astype(jnp.bfloat16)
    out_weight_grad = jnp.einsum(
        "iqhe,iqd->hed",
        combined_heads,
        attended_output_gradient,
        preferred_element_type=jnp.float32,
    )
    mixed_grad = jnp.einsum(
        "iqd,hed->iqhe",
        attended_output_gradient,
        output_complete,
        preferred_element_type=jnp.float32,
    ).astype(jnp.bfloat16)
    scores = scores_of(queries, key_rows, keys_ok, score_scale)
    probs = jnp.exp(scores - logarithm_total)
    probs_low = probs.astype(jnp.bfloat16)
    prob_part = jnp.einsum(
        "iqhe,ikhe->ihqk", mixed_grad, values, preferred_element_type=jnp.float32
    )
    score_grad = (probs * (prob_part - jnp.sum(probs * prob_part, -1, keepdims=True))).astype(
        jnp.bfloat16
    )
    query_grad = (
        jnp.einsum("ihqk,ikhe->iqhe", score_grad, key_rows, preferred_element_type=jnp.float32)
        * score_scale
    )
    key_grad = (
        jnp.einsum("ihqk,iqhe->ikhe", score_grad, queries, preferred_element_type=jnp.float32)
        * score_scale
    )
    value_grad = jnp.einsum(
        "ihqk,iqhe->ikhe", probs_low, mixed_grad, preferred_element_type=jnp.float32
    )
    projected_grad = jnp.concatenate([query_grad, key_grad, value_grad], -1).astype(jnp.bfloat16)
    qkv_grad = jnp.einsum(
        "isd,ishe->dhe", first_in, projected_grad, preferred_element_type=jnp.float32
    )
    first_part = jnp.einsum(
        "ishe,dhe->isd", projected_grad, qkv_full, preferred_element_type=jnp.float32
    )
    first_grad = lax.psum(first_part, "heads")
    input_norm, gain_one_grad = norm_back(
        first_grad, normed_one, spread_one, gain_a.astype(jnp.float32)
    )
    tokens_grad = residual_grad + input_norm
    dense_grads = (
        lax.psum_scatter(qkv_grad, ("fsdp", "tensor"), scatter_dimension=0, tiled=True),
        lax.psum_scatter(out_weight_grad, ("fsdp", "tensor"), scatter_dimension=2, tiled=True),
        lax.psum_scatter(router_grad, ("fsdp", "tensor"), scatter_dimension=0, tiled=True),
        lax.psum_scatter(gain_one_grad, ("fsdp", "tensor"), scatter_dimension=0, tiled=True),
        lax.psum_scatter(gain_two_grad, ("fsdp", "tensor"), scatter_dimension=0, tiled=True),
    )
    expert_grads = reduce_expert_grads(expert_up_grad, expert_down_grad)
    return (
        final.astype(jnp.bfloat16),
        loss_terms,
        tokens_grad,
        dense_grads[3],
        dense_grads[0],
        dense_grads[1],
        dense_grads[4],
        dense_grads[2],
        expert_grads[0],
        expert_grads[1],
    )


def solution(mesh):
    in_specs = (
        P(("fsdp", "tensor"), None, None),
        P(("fsdp", "tensor"), None),
        P("fsdp", None, None),
        P(("fsdp", "tensor"), None, None),
        P(("fsdp", "tensor")),
        P(("fsdp", "tensor"), "heads", None),
        P("heads", None, ("fsdp", "tensor")),
        P(("fsdp", "tensor")),
        P(("fsdp", "tensor"), None),
        P("heads", "fsdp", "tensor"),
        P("heads", "tensor", "fsdp"),
    )
    out_specs = (
        P(("fsdp", "tensor"), None, None),
        P(("fsdp", "tensor")),
        P(("fsdp", "tensor"), None, None),
        P(("fsdp", "tensor")),
        P(("fsdp", "tensor"), "heads", None),
        P("heads", None, ("fsdp", "tensor")),
        P(("fsdp", "tensor")),
        P(("fsdp", "tensor"), None),
        P("heads", "fsdp", "tensor"),
        P("heads", "tensor", "fsdp"),
    )
    return jax.shard_map(local, mesh=mesh, in_specs=in_specs, out_specs=out_specs, check_vma=False)
```

profile of v0, /device:TPU:0, one launch (start us, length us, event | category | flops | bytes accessed | tf_op | source)
XLA Modules:
  0.0 1239.2 jit_solution(9188463020650189161)
XLA Ops:
  8.4 14.6 %all_gather.35 = bf16[768,3,192]{2,1,0:T(4,128)(2,1)S(1)} all-gather(bf16[96,3,192]{2,1,0:T(4,128)(2,1)S(1)} %copy.139), channel_id=1, replica_groups=mesh['fsdp'=2,'heads'=4,'tensor'=4] {'fsdp','tensor'}, dimensions={0}, use_global_device_ids=true | all-gather | bytes 995328 | tf_op jit(solution)/shard_map/all_gather | solution.py:41
  25.8 13.2 %all-reduce.6 = (bf16[768]{0:T(1024)(128)(2,1)S(1)}, bf16[768]{0:T(1024)(128)(2,1)S(1)}) all-reduce(bf16[768]{0:T(1024)(128)(2,1)S(1)} %dynamic-update-slice, bf16[768]{0:T(1024)(128)(2,1)S(1)} %dynamic-update-slice.1), channel_id=1, replica_groups=mesh['fsdp'=2,'heads'=4,'tensor'=4] {'fsdp','tensor'}, use_global_device_ids=true, to_apply=%add | all-reduce | flops 1536 | bytes 6144
  42.2 9.4 all_gather.36
  53.4 44.1 %all-reduce.12.cloned.1.call-done = f32[1,256,768]{2,1,0:T(8,128)} async-done(((f32[1,256,768]{2,1,0:T(8,128)}), f32[1,256,768]{2,1,0:T(8,128)}) %all-reduce.12.cloned.1.call-update) | async-done | bytes 786448 | tf_op jit(solution)/shard_map/psum | solution.py:115
  151.7 87.8 %all-gather.8.cloned.1.call-done = bf16[8,768,768]{2,1,0:T(8,128)(2,1)} async-done(((bf16[8,384,768]{2,1,0:T(8,128)(2,1)}), bf16[8,768,768]{2,1,0:T(8,128)(2,1)}) %all-gather.8.cloned.1.call-update) | async-done | bytes 9437200 | tf_op jit(solution)/shard_map/all_gather | solution.py:48
  254.3 104.6 %all-gather.10.cloned.1.call-done = bf16[8,768,768]{2,1,0:T(8,128)(2,1)} async-done(((bf16[8,768,384]{2,1,0:T(8,128)(2,1)}), bf16[8,768,768]{2,1,0:T(8,128)(2,1)}) %all-gather.10.cloned.1.call-update) | async-done | bytes 9437200 | tf_op jit(solution)/shard_map/all_gather | solution.py:49
  366.0 10.2 gather_fusion.1
  384.4 11.2 multiply_reduce_fusion.1
  395.7 38.0 %reduce-scatter.12.cloned.1.call-done = f32[1,256,768]{2,1,0:T(8,128)} async-done(((f32[4,256,768]{2,1,0:T(8,128)}), f32[1,256,768]{2,1,0:T(8,128)}) %reduce-scatter.12.cloned.1.call-update) | async-done | bytes 786448 | tf_op jit(solution)/shard_map/reduce_scatter | solution.py:160
  434.4 13.3 %psum.44 = f32[]{:T(128)} all-reduce(f32[]{:T(128)} %convert_reduce_fusion.1), channel_id=1, replica_groups=mesh['fsdp'=2,'heads'=4,'tensor'=4] {'fsdp','tensor'}, use_global_device_ids=true, to_apply=%region_20.21 | all-reduce | flops 1 | bytes 8 | tf_op jit(solution)/shard_map/psum | solution.py:74
  448.4 31.4 %all-reduce.14.cloned.1.call-done = f32[1,256,768]{2,1,0:T(8,128)} async-done(((f32[1,256,768]{2,1,0:T(8,128)}), f32[1,256,768]{2,1,0:T(8,128)}) %all-reduce.14.cloned.1.call-update) | async-done | bytes 786448 | tf_op jit(solution)/shard_map/psum | solution.py:159
  482.4 18.9 %all-gather.12.cloned.1.call-done = bf16[4,256,768]{2,1,0:T(8,128)(2,1)} async-done(((bf16[1,256,768]{2,1,0:T(8,128)(2,1)}), bf16[4,256,768]{2,1,0:T(8,128)(2,1)}) %all-gather.12.cloned.1.call-update) | async-done | bytes 1572880 | tf_op jit(solution)/shard_map/all_gather | solution.py:175
  522.4 10.2 gather_fusion.3
  540.7 11.2 multiply_reduce_fusion
  556.3 9.7 gather_fusion.4
  572.8 17.3 %reduce-scatter.14.cloned.1.call-done = f32[1,256,768]{2,1,0:T(8,128)} async-done(((f32[4,256,768]{2,1,0:T(8,128)}), f32[1,256,768]{2,1,0:T(8,128)}) %reduce-scatter.14.cloned.1.call-update) | async-done | bytes 786448 | tf_op jit(solution)/shard_map/reduce_scatter | solution.py:209
  590.8 11.7 psum.46
  604.5 31.7 %all-reduce.16.cloned.1.call-done = f32[1,256,768]{2,1,0:T(8,128)} async-done(((f32[1,256,768]{2,1,0:T(8,128)}), f32[1,256,768]{2,1,0:T(8,128)}) %all-reduce.16.cloned.1.call-update) | async-done | bytes 786448 | tf_op jit(solution)/shard_map/psum | solution.py:212
  674.5 43.9 %all-reduce.18.cloned.1.call-done = f32[1,256,768]{2,1,0:T(8,128)} async-done(((f32[1,256,768]{2,1,0:T(8,128)}), f32[1,256,768]{2,1,0:T(8,128)}) %all-reduce.18.cloned.1.call-update) | async-done | bytes 786448 | tf_op jit(solution)/shard_map/psum | solution.py:275
  720.0 13.8 %all-reduce.5 = (f32[768]{0:T(1024)S(1)}, f32[768]{0:T(1024)S(1)}) all-reduce(f32[768]{0:T(1024)S(1)} %get-tuple-element.14, f32[768]{0:T(1024)S(1)} %copy-done.57), channel_id=5, replica_groups=mesh['fsdp'=2,'heads'=4,'tensor'=4] {'fsdp','tensor'}, use_global_device_ids=true, to_apply=%region_36.37.clone | all-reduce | flops 1536 | bytes 12288
  737.3 18.5 %reduce-scatter.22.cloned.1.call-done = f32[96,192]{1,0:T(8,128)} async-done(((f32[768,192]{1,0:T(8,128)}), f32[96,192]{1,0:T(8,128)}) %reduce-scatter.22.cloned.1.call-update) | async-done | bytes 73744
  757.6 44.6 %reduce-scatter.16.cloned.1.call-done = f32[96,3,192]{2,0,1:T(8,128)} async-done(((f32[768,3,192]{2,0,1:T(8,128)}), f32[96,3,192]{2,0,1:T(8,128)}) %reduce-scatter.16.cloned.1.call-update) | async-done | bytes 221200 | tf_op jit(solution)/shard_map/reduce_scatter | solution.py:281
  802.2 214.5 %reduce-scatter.18.cloned.1.call-done = f32[8,384,768]{2,1,0:T(8,128)} async-done(((f32[8,768,768]{2,1,0:T(8,128)}), f32[8,384,768]{2,1,0:T(8,128)}) %reduce-scatter.18.cloned.1.call-update) | async-done | bytes 9437200 | tf_op jit(solution)/shard_map/reduce_scatter | solution.py:56
  1016.8 214.5 %reduce-scatter.20.cloned.1.call-done = f32[8,768,384]{2,1,0:T(8,128)} async-done(((f32[8,768,768]{2,1,0:T(8,128)}), f32[8,768,384]{2,1,0:T(8,128)}) %reduce-scatter.20.cloned.1.call-update) | async-done | bytes 9437200 | tf_op jit(solution)/shard_map/reduce_scatter | solution.py:57
  (276 shorter events, 180.9 us)
Async XLA Ops:
  7.2 90.3 %all-reduce.12.cloned.1.call-start = ((), (), s32[]{:S(2)}) async-start(), calls=%async_computation.7 | async-start | bytes 1572864 | tf_op jit(solution)/shard_map/psum | solution.py:115
  53.3 80.5 %all-gather.6.cloned.1.call-start = ((), (), s32[]{:S(2)}) async-start(), calls=%async_computation.8 | async-start | bytes 1966080 | tf_op jit(solution)/shard_map/all_gather | solution.py:119
  100.7 138.8 %all-gather.8.cloned.1.call-start = ((), (), s32[]{:S(2)}) async-start(), calls=%async_computation.9 | async-start | bytes 14155776 | tf_op jit(solution)/shard_map/all_gather | solution.py:48
  101.5 257.5 %all-gather.10.cloned.1.call-start = ((), (), s32[]{:S(2)}) async-start(), calls=%async_computation.10 | async-start | bytes 14155776 | tf_op jit(solution)/shard_map/all_gather | solution.py:49
  102.1 331.6 %reduce-scatter.12.cloned.1.call-start = ((), (), s32[]{:S(2)}) async-start(), calls=%async_computation.11 | async-start | bytes 3932160 | tf_op jit(solution)/shard_map/reduce_scatter | solution.py:160
  140.3 105.3 %copy-start.17 = (bf16[1024,768]{1,0:T(8,128)(2,1)}, bf16[1024,768]{1,0:T(8,128)(2,1)S(1)}, u32[]{:S(2)}) copy-start(bf16[1024,768]{1,0:T(8,128)(2,1)S(1)} %gather_fusion) | copy-start | bytes 4718596
  151.7 355.8 %copy-start.44 = (f32[1024]{0:T(1024)}, f32[1024]{0:T(1024)S(1)}, u32[]{:S(2)}) copy-start(f32[1024]{0:T(1024)S(1)} %scatter_custom_fusion.1) | copy-start | bytes 12292
  254.3 104.6 %copy-start.8 = (bf16[8,128,768]{2,1,0:T(8,128)(2,1)}, bf16[8,128,768]{2,1,0:T(8,128)(2,1)S(1)}, u32[]{:S(2)}) copy-start(bf16[8,128,768]{2,1,0:T(8,128)(2,1)S(1)} %fusion.4) | copy-start | bytes 4718596
  395.6 84.2 %copy-start.4 = (f32[1,256,768]{2,1,0:T(8,128)S(1)}, f32[1,256,768]{2,1,0:T(8,128)}, u32[]{:S(2)}) copy-start(f32[1,256,768]{2,1,0:T(8,128)} %copy-done.3) | copy-start | bytes 2359300
  395.6 84.2 %copy-start.35 = (bf16[1,256,768]{2,1,0:T(8,128)(2,1)S(1)}, bf16[1,256,768]{2,1,0:T(8,128)(2,1)}, u32[]{:S(2)}) copy-start(bf16[1,256,768]{2,1,0:T(8,128)(2,1)} %param.14) | copy-start | bytes 1179652
  395.6 105.8 %copy-start.47 = (s32[1024]{0:T(1024)S(1)}, s32[1024]{0:T(1024)}, u32[]{:S(2)}) copy-start(s32[1024]{0:T(1024)} %copy-done.46) | copy-start | bytes 12292
  395.6 84.1 %all-reduce.14.cloned.1.call-start = ((), (), s32[]{:S(2)}) async-start(), calls=%async_computation.12 | async-start | bytes 1572864 | tf_op jit(solution)/shard_map/psum | solution.py:159
  433.7 67.6 %all-gather.12.cloned.1.call-start = ((), (), s32[]{:S(2)}) async-start(), calls=%async_computation.13 | async-start | bytes 1966080 | tf_op jit(solution)/shard_map/all_gather | solution.py:175
  482.2 107.9 %reduce-scatter.14.cloned.1.call-start = ((), (), s32[]{:S(2)}) async-start(), calls=%async_computation.14 | async-start | bytes 3932160 | tf_op jit(solution)/shard_map/reduce_scatter | solution.py:209
  552.0 84.3 %all-reduce.16.cloned.1.call-start = ((), (), s32[]{:S(2)}) async-start(), calls=%async_computation.15 | async-start | bytes 1572864 | tf_op jit(solution)/shard_map/psum | solution.py:212
  566.0 70.2 %copy-start.5 = (f32[1,256,768]{2,1,0:T(8,128)S(1)}, f32[1,256,768]{2,1,0:T(8,128)}, u32[]{:S(2)}) copy-start(f32[1,256,768]{2,1,0:T(8,128)} %copy-done.3) | copy-start | bytes 2359300
  566.0 70.2 %copy-start.31 = (bf16[768,32]{0,1:T(8,128)(2,1)S(1)}, bf16[768,32]{0,1:T(8,128)(2,1)}, u32[]{:S(2)}) copy-start(bf16[768,32]{0,1:T(8,128)(2,1)} %reshape.512) | copy-start | bytes 147460
  566.1 72.4 %copy-start.23 = (f32[1,256,768]{2,1,0:T(8,128)S(1)}, f32[1,256,768]{2,1,0:T(8,128)}, u32[]{:S(2)}) copy-start(f32[1,256,768]{2,1,0:T(8,128)} %get-tuple-element.23) | copy-start | bytes 2359300
  590.1 82.3 %reduce-scatter.24.cloned.1.call-start = ((), (), s32[]{:S(2)}) async-start(), calls=%async_computation.21 | async-start | bytes 442368
  604.5 114.0 %all-reduce.18.cloned.1.call-start = ((), (), s32[]{:S(2)}) async-start(), calls=%async_computation.16 | async-start | bytes 1572864 | tf_op jit(solution)/shard_map/psum | solution.py:275
  644.4 111.4 %reduce-scatter.22.cloned.1.call-start = ((), (), s32[]{:S(2)}) async-start(), calls=%async_computation.20 | async-start | bytes 884736
  647.5 154.8 %reduce-scatter.16.cloned.1.call-start = ((), (), s32[]{:S(2)}) async-start(), calls=%async_computation.17 | async-start | bytes 2654208 | tf_op jit(solution)/shard_map/reduce_scatter | solution.py:281
  650.8 366.0 %reduce-scatter.18.cloned.1.call-start = ((), (), s32[]{:S(2)}) async-start(), calls=%async_computation.18 | async-start | bytes 28311552 | tf_op jit(solution)/shard_map/reduce_scatter | solution.py:56
  658.8 572.4 %reduce-scatter.20.cloned.1.call-start = ((), (), s32[]{:S(2)}) async-start(), calls=%async_computation.19 | async-start | bytes 28311552 | tf_op jit(solution)/shard_map/reduce_scatter | solution.py:57
  (57 other events, 902.5 us)
Sparse Core Ops, SparseCore 0:
  53.4 44.0 all-reduce.11
  100.8 18.9 all-gather.5
  121.4 118.0 all-gather.7
  240.9 117.9 all-gather.9
  395.7 37.9 reduce-scatter.11
  436.0 43.6 all-reduce.13
  482.3 18.9 all-gather.11
  552.1 37.9 reduce-scatter.13
  592.5 43.6 all-reduce.15
  639.1 33.2 reduce-scatter.23
  674.8 43.6 all-reduce.17
  721.5 34.2 reduce-scatter.21
  759.7 42.4 reduce-scatter.15
  805.1 211.6 reduce-scatter.17
  1019.6 211.6 reduce-scatter.19
where the time goes:
time: 1250 us; the launch traced here: 1240 us
  waiting for transfers between devices  914 us (73%)
  local copies, waits for them, and re-layouts  102 us (8%)
  blocking collectives  91.2 us (7%)
  other arithmetic  55.8 us (4%)
  matrix products  55.2 us (4%)
  between operations  19.8 us (2%)
    reduce_scatter x1, waiting for transfers between devices, reduce_expert_grads(): lax.psum_scatter(up_grad, 'fsdp', scatter_dimension=1, tiled=True)  215 us
    reduce_scatter x1, waiting for transfers between devices, reduce_expert_grads(): lax.psum_scatter(down_grad, 'fsdp', scatter_dimension=2, tiled=True)  215 us
    all_gather x1, waiting for transfers between devices, gather_weights(): lax.all_gather(expert_down, 'fsdp', axis=2, tiled=True)  105 us
    all_gather x1, waiting for transfers between devices, gather_weights(): lax.all_gather(expert_up, 'fsdp', axis=1, tiled=True)  87.8 us
    reduce_scatter x1, waiting for transfers between devices, local(): lax.psum_scatter(qkv_grad, ('fsdp', 'tensor'), scatter_dimension=0, tiled...  44.6 us
    psum x1, waiting for transfers between devices, local(): attended = lax.psum(attn_part, 'heads')  44.1 us
    psum x1, waiting for transfers between devices, local(): first_grad = lax.psum(first_part, 'heads')  43.9 us
    reduce_scatter x1, waiting for transfers between devices, local(): lax.psum_scatter(moe_part, 'tensor', scatter_dimension=0, tiled=True)  38 us
  transfers between devices with their start and end apart: 15, of which 14 were waited for; matrix products, arithmetic and copies ran while one was open for 9% of the time, Pallas kernels for 0%

commit v1 on v0

--- a/solution.py
+++ b/solution.py
@@ -272,7 +272,10 @@
     first_part = jnp.einsum(
         "ishe,dhe->isd", projected_grad, qkv_full, preferred_element_type=jnp.float32
     )
-    first_grad = lax.psum(first_part, "heads")
+    size, first_grad = (lax.axis_size("heads"), first_part)
+    for far in [1 << k for k in range(size.bit_length() - 1)]:
+        route = [(i, i ^ far) for i in range(size)]
+        first_grad = first_grad + lax.ppermute(first_grad, "heads", route)
     input_norm, gain_one_grad = norm_back(
         first_grad, normed_one, spread_one, gain_a.astype(jnp.float32)
     )

time: 1250 us -> 1200 us (0.960)
  waiting for transfers between devices: 914 us -> 860 us
    psum x1 -> x0, waiting for transfers between devices: 43.9 us -> none  [local(): first_grad = lax.psum(first_part, 'heads')]
    reduce_scatter x1, waiting for transfers between devices: 44.6 us -> 8.27 us  [local(): lax.psum_scatter(qkv_grad, ('fsdp', 'tensor'), scatter_dimension=0, tiled...]
    ppermute x0 -> x2, waiting for transfers between devices: none -> 35.8 us  [local(): first_grad = first_grad + lax.ppermute(first_grad, 'heads', route)]
  transfers between devices with their start and end apart: 15 -> 16, of which waited for: 14 -> 14; matrix products, arithmetic and copies ran while one was open for 9% -> 9% of each run, Pallas kernels for 0% -> 0%
where the time goes in v1:
time: 1200 us; the launch traced here: 1190 us
  waiting for transfers between devices  860 us (72%)
  local copies, waits for them, and re-layouts  105 us (9%)
  blocking collectives  91.4 us (8%)
  matrix products  59.1 us (5%)
  other arithmetic  55.5 us (5%)
  between operations  19.7 us (2%)
    reduce_scatter x1, waiting for transfers between devices, reduce_expert_grads(): lax.psum_scatter(up_grad, 'fsdp', scatter_dimension=1, tiled=True)  215 us
    reduce_scatter x1, waiting for transfers between devices, reduce_expert_grads(): lax.psum_scatter(down_grad, 'fsdp', scatter_dimension=2, tiled=True)  215 us
    all_gather x1, waiting for transfers between devices, gather_weights(): lax.all_gather(expert_down, 'fsdp', axis=2, tiled=True)  105 us
    all_gather x1, waiting for transfers between devices, gather_weights(): lax.all_gather(expert_up, 'fsdp', axis=1, tiled=True)  87.8 us
    psum x1, waiting for transfers between devices, local(): attended = lax.psum(attn_part, 'heads')  44.1 us
    reduce_scatter x1, waiting for transfers between devices, local(): lax.psum_scatter(moe_part, 'tensor', scatter_dimension=0, tiled=True)  38 us
    ppermute x2, waiting for transfers between devices, local(): first_grad = first_grad + lax.ppermute(first_grad, 'heads', route)  35.8 us
    unnamed x3, blocking collectives  33.2 us
  transfers between devices with their start and end apart: 16, of which 14 were waited for; matrix products, arithmetic and copies ran while one was open for 9% of the time, Pallas kernels for 0%

profile of v1, /device:TPU:0, one launch (start us, length us, event | category | flops | bytes accessed | tf_op | source)
XLA Modules:
  0.0 1194.2 jit_solution(9269272417598960800)
XLA Ops:
  8.4 14.6 %all_gather.35 = bf16[768,3,192]{2,1,0:T(4,128)(2,1)S(1)} all-gather(bf16[96,3,192]{2,1,0:T(4,128)(2,1)S(1)} %copy.139), channel_id=1, replica_groups=mesh['fsdp'=2,'heads'=4,'tensor'=4] {'fsdp','tensor'}, dimensions={0}, use_global_device_ids=true | all-gather | bytes 995328 | tf_op jit(solution)/shard_map/all_gather | solution.py:41
  25.8 13.2 %all-reduce.6 = (bf16[768]{0:T(1024)(128)(2,1)S(1)}, bf16[768]{0:T(1024)(128)(2,1)S(1)}) all-reduce(bf16[768]{0:T(1024)(128)(2,1)S(1)} %dynamic-update-slice, bf16[768]{0:T(1024)(128)(2,1)S(1)} %dynamic-update-slice.1), channel_id=1, replica_groups=mesh['fsdp'=2,'heads'=4,'tensor'=4] {'fsdp','tensor'}, use_global_device_ids=true, to_apply=%add | all-reduce | flops 1536 | bytes 6144
  53.5 44.1 %all-reduce.11.cloned.1.call-done = f32[1,256,768]{2,1,0:T(8,128)} async-done(((f32[1,256,768]{2,1,0:T(8,128)}), f32[1,256,768]{2,1,0:T(8,128)}) %all-reduce.11.cloned.1.call-update) | async-done | bytes 786448 | tf_op jit(solution)/shard_map/psum | solution.py:115
  151.8 87.8 %all-gather.8.cloned.1.call-done = bf16[8,768,768]{2,1,0:T(8,128)(2,1)} async-done(((bf16[8,384,768]{2,1,0:T(8,128)(2,1)}), bf16[8,768,768]{2,1,0:T(8,128)(2,1)}) %all-gather.8.cloned.1.call-update) | async-done | bytes 9437200 | tf_op jit(solution)/shard_map/all_gather | solution.py:48
  254.4 104.6 %all-gather.10.cloned.1.call-done = bf16[8,768,768]{2,1,0:T(8,128)(2,1)} async-done(((bf16[8,768,384]{2,1,0:T(8,128)(2,1)}), bf16[8,768,768]{2,1,0:T(8,128)(2,1)}) %all-gather.10.cloned.1.call-update) | async-done | bytes 9437200 | tf_op jit(solution)/shard_map/all_gather | solution.py:49
  366.1 10.2 gather_fusion.1
  384.5 11.2 multiply_reduce_fusion.1
  395.7 38.0 %reduce-scatter.12.cloned.1.call-done = f32[1,256,768]{2,1,0:T(8,128)} async-done(((f32[4,256,768]{2,1,0:T(8,128)}), f32[1,256,768]{2,1,0:T(8,128)}) %reduce-scatter.12.cloned.1.call-update) | async-done | bytes 786448 | tf_op jit(solution)/shard_map/reduce_scatter | solution.py:160
  434.4 13.3 %psum.37 = f32[]{:T(128)} all-reduce(f32[]{:T(128)} %convert_reduce_fusion.1), channel_id=1, replica_groups=mesh['fsdp'=2,'heads'=4,'tensor'=4] {'fsdp','tensor'}, use_global_device_ids=true, to_apply=%region_20.21 | all-reduce | flops 1 | bytes 8 | tf_op jit(solution)/shard_map/psum | solution.py:74
  448.4 31.4 %all-reduce.13.cloned.1.call-done = f32[1,256,768]{2,1,0:T(8,128)} async-done(((f32[1,256,768]{2,1,0:T(8,128)}), f32[1,256,768]{2,1,0:T(8,128)}) %all-reduce.13.cloned.1.call-update) | async-done | bytes 786448 | tf_op jit(solution)/shard_map/psum | solution.py:159
  482.5 18.9 %all-gather.12.cloned.1.call-done = bf16[4,256,768]{2,1,0:T(8,128)(2,1)} async-done(((bf16[1,256,768]{2,1,0:T(8,128)(2,1)}), bf16[4,256,768]{2,1,0:T(8,128)(2,1)}) %all-gather.12.cloned.1.call-update) | async-done | bytes 1572880 | tf_op jit(solution)/shard_map/all_gather | solution.py:175
  522.4 10.2 gather_fusion.3
  540.8 11.2 multiply_reduce_fusion
  556.4 9.7 gather_fusion.4
  572.9 17.4 %reduce-scatter.14.cloned.1.call-done = f32[1,256,768]{2,1,0:T(8,128)} async-done(((f32[4,256,768]{2,1,0:T(8,128)}), f32[1,256,768]{2,1,0:T(8,128)}) %reduce-scatter.14.cloned.1.call-update) | async-done | bytes 786448 | tf_op jit(solution)/shard_map/reduce_scatter | solution.py:209
  591.0 11.7 psum.39
  604.6 31.7 %all-reduce.15.cloned.1.call-done = f32[1,256,768]{2,1,0:T(8,128)} async-done(((f32[1,256,768]{2,1,0:T(8,128)}), f32[1,256,768]{2,1,0:T(8,128)}) %all-reduce.15.cloned.1.call-update) | async-done | bytes 786448 | tf_op jit(solution)/shard_map/psum | solution.py:212
  652.4 10.5 fusion.82
  675.8 18.0 %collective-permute-done = f32[1,256,768]{2,1,0:T(8,128)S(1)} collective-permute-done((f32[1,256,768]{2,1,0:T(8,128)S(1)}, f32[1,256,768]{2,1,0:T(8,128)S(1)}, u32[]{:S(2)}, u32[]{:S(2)}) %collective-permute-start) | collective-permute-done | bytes 786464 | tf_op jit(solution)/shard_map/ppermute | solution.py:278
  699.0 11.5 reduce-scatter.22.cloned.1.call-done
  712.4 17.8 %collective-permute-done.1 = f32[1,256,768]{2,1,0:T(8,128)S(1)} collective-permute-done((f32[1,256,768]{2,1,0:T(8,128)S(1)}, f32[1,256,768]{2,1,0:T(8,128)S(1)}, u32[]{:S(2)}, u32[]{:S(2)}) %collective-permute-start.1) | collective-permute-done | bytes 786464 | tf_op jit(solution)/shard_map/ppermute | solution.py:278
  731.1 13.9 %all-reduce.5 = (f32[768]{0:T(1024)S(1)}, f32[768]{0:T(1024)S(1)}) all-reduce(f32[768]{0:T(1024)} %get-tuple-element.14, f32[768]{0:T(1024)S(1)} %copy-done.60), channel_id=5, replica_groups=mesh['fsdp'=2,'heads'=4,'tensor'=4] {'fsdp','tensor'}, use_global_device_ids=true, to_apply=%region_35.36.clone | all-reduce | flops 1536 | bytes 12288
  757.1 214.7 %reduce-scatter.18.cloned.1.call-done = f32[8,384,768]{2,1,0:T(8,128)} async-done(((f32[8,768,768]{2,1,0:T(8,128)}), f32[8,384,768]{2,1,0:T(8,128)}) %reduce-scatter.18.cloned.1.call-update) | async-done | bytes 9437200 | tf_op jit(solution)/shard_map/reduce_scatter | solution.py:56
  971.7 214.6 %reduce-scatter.20.cloned.1.call-done = f32[8,768,384]{2,1,0:T(8,128)} async-done(((f32[8,768,768]{2,1,0:T(8,128)}), f32[8,768,384]{2,1,0:T(8,128)}) %reduce-scatter.20.cloned.1.call-update) | async-done | bytes 9437200 | tf_op jit(solution)/shard_map/reduce_scatter | solution.py:57
  (284 shorter events, 194.3 us)
Async XLA Ops:
  7.2 90.4 %all-reduce.11.cloned.1.call-start = ((), (), s32[]{:S(2)}) async-start(), calls=%async_computation.7 | async-start | bytes 1572864 | tf_op jit(solution)/shard_map/psum | solution.py:115
  53.4 80.5 %all-gather.6.cloned.1.call-start = ((), (), s32[]{:S(2)}) async-start(), calls=%async_computation.8 | async-start | bytes 1966080 | tf_op jit(solution)/shard_map/all_gather | solution.py:119
  100.8 138.8 %all-gather.8.cloned.1.call-start = ((), (), s32[]{:S(2)}) async-start(), calls=%async_computation.9 | async-start | bytes 14155776 | tf_op jit(solution)/shard_map/all_gather | solution.py:48
  101.5 257.5 %all-gather.10.cloned.1.call-start = ((), (), s32[]{:S(2)}) async-start(), calls=%async_computation.10 | async-start | bytes 14155776 | tf_op jit(solution)/shard_map/all_gather | solution.py:49
  102.1 331.6 %reduce-scatter.12.cloned.1.call-start = ((), (), s32[]{:S(2)}) async-start(), calls=%async_computation.11 | async-start | bytes 3932160 | tf_op jit(solution)/shard_map/reduce_scatter | solution.py:160
  140.4 105.3 %copy-start.17 = (bf16[1024,768]{1,0:T(8,128)(2,1)}, bf16[1024,768]{1,0:T(8,128)(2,1)S(1)}, u32[]{:S(2)}) copy-start(bf16[1024,768]{1,0:T(8,128)(2,1)S(1)} %gather_fusion) | copy-start | bytes 4718596
  151.8 355.8 %copy-start.46 = (f32[1024]{0:T(1024)}, f32[1024]{0:T(1024)S(1)}, u32[]{:S(2)}) copy-start(f32[1024]{0:T(1024)S(1)} %scatter_custom_fusion.1) | copy-start | bytes 12292
  254.4 104.6 %copy-start.8 = (bf16[8,128,768]{2,1,0:T(8,128)(2,1)}, bf16[8,128,768]{2,1,0:T(8,128)(2,1)S(1)}, u32[]{:S(2)}) copy-start(bf16[8,128,768]{2,1,0:T(8,128)(2,1)S(1)} %fusion.4) | copy-start | bytes 4718596
  395.6 84.2 %copy-start.4 = (f32[1,256,768]{2,1,0:T(8,128)S(1)}, f32[1,256,768]{2,1,0:T(8,128)}, u32[]{:S(2)}) copy-start(f32[1,256,768]{2,1,0:T(8,128)} %copy-done.3) | copy-start | bytes 2359300
  395.6 84.2 %copy-start.34 = (bf16[1,256,768]{2,1,0:T(8,128)(2,1)S(1)}, bf16[1,256,768]{2,1,0:T(8,128)(2,1)}, u32[]{:S(2)}) copy-start(bf16[1,256,768]{2,1,0:T(8,128)(2,1)} %param.14) | copy-start | bytes 1179652
  395.7 105.8 %copy-start.49 = (s32[1024]{0:T(1024)S(1)}, s32[1024]{0:T(1024)}, u32[]{:S(2)}) copy-start(s32[1024]{0:T(1024)} %copy-done.48) | copy-start | bytes 12292
  395.7 84.1 %all-reduce.13.cloned.1.call-start = ((), (), s32[]{:S(2)}) async-start(), calls=%async_computation.12 | async-start | bytes 1572864 | tf_op jit(solution)/shard_map/psum | solution.py:159
  433.8 67.6 %all-gather.12.cloned.1.call-start = ((), (), s32[]{:S(2)}) async-start(), calls=%async_computation.13 | async-start | bytes 1966080 | tf_op jit(solution)/shard_map/all_gather | solution.py:175
  482.3 108.0 %reduce-scatter.14.cloned.1.call-start = ((), (), s32[]{:S(2)}) async-start(), calls=%async_computation.14 | async-start | bytes 3932160 | tf_op jit(solution)/shard_map/reduce_scatter | solution.py:209
  552.0 84.3 %all-reduce.15.cloned.1.call-start = ((), (), s32[]{:S(2)}) async-start(), calls=%async_computation.15 | async-start | bytes 1572864 | tf_op jit(solution)/shard_map/psum | solution.py:212
  566.2 72.4 %copy-start.22 = (f32[1,256,768]{2,1,0:T(8,128)S(1)}, f32[1,256,768]{2,1,0:T(8,128)}, u32[]{:S(2)}) copy-start(f32[1,256,768]{2,1,0:T(8,128)} %get-tuple-element.24) | copy-start | bytes 2359300
  590.3 106.6 %reduce-scatter.24.cloned.1.call-start = ((), (), s32[]{:S(2)}) async-start(), calls=%async_computation.20 | async-start | bytes 442368
  604.6 106.0 %reduce-scatter.22.cloned.1.call-start = ((), (), s32[]{:S(2)}) async-start(), calls=%async_computation.19 | async-start | bytes 884736
  649.2 107.9 %reduce-scatter.16.cloned.1.call-start = ((), (), s32[]{:S(2)}) async-start(), calls=%async_computation.16 | async-start | bytes 2654208 | tf_op jit(solution)/shard_map/reduce_scatter | solution.py:284
  652.4 319.4 %reduce-scatter.18.cloned.1.call-start = ((), (), s32[]{:S(2)}) async-start(), calls=%async_computation.17 | async-start | bytes 28311552 | tf_op jit(solution)/shard_map/reduce_scatter | solution.py:56
  663.0 523.3 %reduce-scatter.20.cloned.1.call-start = ((), (), s32[]{:S(2)}) async-start(), calls=%async_computation.18 | async-start | bytes 28311552 | tf_op jit(solution)/shard_map/reduce_scatter | solution.py:57
  674.5 73.1 %copy-start.14 = (f32[1,256,768]{2,1,0:T(8,128)S(1)}, f32[1,256,768]{2,1,0:T(8,128)}, u32[]{:S(2)}) copy-start(f32[1,256,768]{2,1,0:T(8,128)} %copy-done.13) | copy-start | bytes 2359300
  674.5 19.3 %collective-permute-start = (f32[1,256,768]{2,1,0:T(8,128)S(1)}, f32[1,256,768]{2,1,0:T(8,128)S(1)}, u32[]{:S(2)}, u32[]{:S(2)}) collective-permute-start(f32[1,256,768]{2,1,0:T(8,128)S(1)} %convolution_bitcast_fusion), channel_id=1, source_target_pairs={{0,4},{4,0},{8,12},{12,8},{1,5},{5,1},{9,13},{13,9},{2,6},{6,2},{1... | collective-permute-start | bytes 2359304 | tf_op jit(solution)/shard_map/ppermute | solution.py:278
  693.9 36.2 %collective-permute-start.1 = (f32[1,256,768]{2,1,0:T(8,128)S(1)}, f32[1,256,768]{2,1,0:T(8,128)S(1)}, u32[]{:S(2)}, u32[]{:S(2)}) collective-permute-start(f32[1,256,768]{2,1,0:T(8,128)S(1)} %add.145), channel_id=1, source_target_pairs={{0,8},{4,12},{8,0},{12,4},{1,9},{5,13},{9,1},{13,5},{2,10},{6,14},... | collective-permute-start | bytes 2359304 | tf_op jit(solution)/shard_map/ppermute | solution.py:278
  (61 other events, 1016.4 us)
Sparse Core Ops, SparseCore 0:
  53.5 44.0 all-reduce.10
  100.9 18.9 all-gather.5
  121.5 118.0 all-gather.7
  241.0 117.9 all-gather.9
  395.8 37.9 reduce-scatter.11
  436.1 43.6 all-reduce.12
  482.4 18.9 all-gather.11
  552.1 38.0 reduce-scatter.13
  592.6 43.6 all-reduce.14
  639.2 33.1 reduce-scatter.23
  675.6 34.9 reduce-scatter.21
  714.4 42.6 reduce-scatter.15
  760.1 211.6 reduce-scatter.17
  974.6 211.6 reduce-scatter.19
